TPU v7x, 32 devices: a whole 2x2x4 slice. The times are simulated.
32 devices in a mesh: groups: 2 (over y), ctx: 4 (over z), head: 4 (over x, core).
Axes of the slice: x: 2, y: 2, z: 4, core: 2. Of those that a mesh axis runs over, the one named last changes fastest.
Arguments:
- hidden: bfloat16 [1024, 7168], P(('groups', 'ctx'), 'head'), parts along dimension 0, may hold values from -210 to 210
- q_latent: bfloat16 [1024, 1536], P(('groups', 'ctx')), parts along dimension 0, may hold values from -210 to 210
- w_down: bfloat16 [7168, 576], P('head'), may hold values from -0.0625 to 0.0625
- latent_gain: float32 [512], replicated, may hold values from 0.1 to 1.9
- w_qup: bfloat16 [1536, 12288], P(None, 'head'), may hold values from -0.15625 to 0.15625
- w_kvup: bfloat16 [512, 16384], P(None, 'head'), may hold values from -0.25 to 0.25
- w_out: bfloat16 [8192, 7168], P('head', 'ctx'), may hold values from -0.0625 to 0.0625
Outputs:
- mixed: bfloat16 [1024, 7168], P(('groups', 'head'), 'ctx'), parts along dimension 0
There are 2 independent parts, one for each index of `groups`. A program takes and returns all parts, laid end to end along the dimension named above; an argument that names none is the same for every part. Nothing has to cross between parts.
All inputs are finite; a program needn't handle non-finite values.
Results may differ from a plain program's by a relative error of at most 0.012.
The roundings to bfloat16 on the way count: a program that leaves them out, or rounds other values in their place, can miss the bound.
Values may be sent and summed in bfloat16 or wider, within the bound.
A program may use at most 128 MiB of HBM per device.

v0:
```python
import math

import jax
import jax.numpy as jnp
from jax import lax
from jax.sharding import PartitionSpec as P

NOPE = 128
ROPE = 64
VDIM = 128
KVRANK = 512


def rotate(pairs, position):
    half = pairs.shape[-1] // 2
    freqs = jnp.exp(
        jnp.arange(half, dtype=jnp.float32) * (-2.0 * math.log(10000.0) / pairs.shape[-1])
    )
    angle = position[..., None] * freqs
    first_half = pairs[..., :half]
    second_half = pairs[..., half:]
    return jnp.concatenate(
        [
            first_half * jnp.cos(angle) - second_half * jnp.sin(angle),
            first_half * jnp.sin(angle) + second_half * jnp.cos(angle),
        ],
        -1,
    )


def finish(compressed, position, latent_gain):
    lat_part = compressed[:, :KVRANK]
    latent = (
        lat_part * lax.rsqrt(jnp.mean(lat_part * lat_part, -1, keepdims=True) + 1e-06) * latent_gain
    ).astype(jnp.bfloat16)
    rope_key = rotate(compressed[:, KVRANK:], position).astype(jnp.bfloat16)
    return (latent, rope_key)


def body(hidden, q_latent, w_down, latent_gain, w_qup, w_kvup, w_out):
    tok_count = q_latent.shape[0]
    first = lax.axis_index("ctx") * tok_count
    token_index = first + jnp.arange(tok_count, dtype=jnp.int32)
    position = token_index.astype(jnp.float32)
    partial_sum = jnp.dot(hidden, w_down, preferred_element_type=jnp.float32)
    compressed = lax.psum(partial_sum, "head")
    latent, rope_key = finish(compressed, position, latent_gain)
    width = NOPE + ROPE
    heads_here = w_qup.shape[1] // width
    query = jnp.dot(q_latent, w_qup, preferred_element_type=jnp.float32).reshape(
        tok_count, heads_here, width
    )
    query = jnp.concatenate(
        [query[..., :NOPE], rotate(query[..., NOPE:], position[:, None])], -1
    ).astype(jnp.bfloat16)
    scale = (NOPE + ROPE) ** (-0.5)
    last_index = first + tok_count - 1
    init = (
        jnp.full((heads_here, tok_count), -1e30, jnp.float32),
        jnp.zeros((heads_here, tok_count), jnp.float32),
        jnp.zeros((tok_count, heads_here, VDIM), jnp.float32),
    )
    keyval_local = jnp.dot(latent, w_kvup, preferred_element_type=jnp.float32).astype(jnp.bfloat16)
    keyval = lax.all_gather(keyval_local, "ctx", axis=0, tiled=True)
    rope_piece = lax.all_gather(rope_key, "ctx", axis=0, tiled=True)

    def compute(state):
        best, total, accum = state
        keys_count = rope_piece.shape[0]
        grouped = keyval.reshape(keys_count, heads_here, NOPE + VDIM)
        scores = jnp.einsum(
            "thd,nhd->htn",
            query[..., :NOPE],
            grouped[..., :NOPE],
            preferred_element_type=jnp.float32,
        )
        scores = scores + jnp.einsum(
            "thr,nr->htn", query[..., NOPE:], rope_piece, preferred_element_type=jnp.float32
        )
        key_index = jnp.arange(keys_count, dtype=jnp.int32)
        allowed = (key_index[None, :] <= token_index[:, None])[None]
        scores = jnp.where(allowed, scores * scale, -1e30)
        new_best = jnp.maximum(best, jnp.max(scores, -1))
        probs = jnp.where(allowed, jnp.exp(scores - new_best[..., None]), 0.0)
        factor = jnp.exp(best - new_best)
        total = jnp.sum(probs, -1)
        weights = probs.astype(jnp.bfloat16)
        accum = accum * factor.T[..., None] + jnp.einsum(
            "htn,nhv->thv", weights, grouped[..., NOPE:], preferred_element_type=jnp.float32
        )
        return (new_best, total, accum)

    def keep(state):
        return state

    best, total, accum = lax.cond(jnp.int32(0) <= last_index, compute, keep, init)
    attended = (
        (accum / total.T[..., None]).astype(jnp.bfloat16).reshape(tok_count, heads_here * VDIM)
    )
    terms = jnp.dot(
        lax.all_gather(attended, "ctx", axis=0, tiled=True),
        w_out,
        preferred_element_type=jnp.float32,
    )
    return lax.psum_scatter(terms.astype(jnp.bfloat16), "head", scatter_dimension=0, tiled=True)


def solution(mesh):
    in_specs = (
        P(("groups", "ctx"), "head"),
        P(("groups", "ctx"), None),
        P("head", None),
        P(),
        P(None, "head"),
        P(None, "head"),
        P("head", "ctx"),
    )
    out_specs = P(("groups", "head"), "ctx")
    return jax.shard_map(body, mesh=mesh, in_specs=in_specs, out_specs=out_specs, check_vma=False)
```

profile of v0, /device:TPU:11, one launch (start us, length us, event | category | flops | bytes accessed | tf_op | source)
XLA Modules:
  0.0 237.3 jit_solution(16711507275087998460)
XLA Ops:
  6.5 0.0 copy-start
  6.5 0.0 all-reduce.2.cloned.1.call-start
  6.5 1.6 copy-done
  8.1 2.4 %fusion.30 = f32[128,576]{0,1:T(8,128)} fusion(bf16[128,1792]{1,0:T(8,128)(2,1)} %param.9, bf16[1792,576]{0,1:T(8,128)(2,1)S(1)} %copy-done), kind=kOutput, calls=%fused_computation.44 | convolution fusion | flops 264241152 | bytes 2818048 | tf_op jit(solution)/shard_map/dot_general | solution.py:45
  10.5 0.0 copy-start.2
  10.5 0.0 all-reduce.2.cloned.1.call-update
  10.6 0.0 all-gather.3.cloned.1.call-start
  10.6 31.9 %all-reduce.2.cloned.1.call-done = f32[128,576]{0,1:T(8,128)} async-done(((f32[128,576]{0,1:T(8,128)}), f32[128,576]{0,1:T(8,128)}) %all-reduce.2.cloned.1.call-update) | async-done | bytes 294928 | tf_op jit(solution)/shard_map/psum | solution.py:46
  42.6 1.0 multiply_reduce_fusion
  43.6 4.1 %convolution_convert_fusion = bf16[128,4096]{1,0:T(8,128)(2,1)} fusion(bf16[512,4096]{1,0:T(8,128)(2,1)} %param.14, f32[128,576]{0,1:T(8,128)} %all-reduce.2.cloned.1.call-done, f32[512]{0:T(512)} %param.12, f32[128]{0:T(128)S(1)} %add_rsqrt_fusion), kind=kOutput, calls=%fused_computation.23 | convolution fusion | flops 537591808 | bytes 5507584 | tf_op jit(solution)/shard_map/dot_general | solution.py:63
  47.7 0.0 all-gather.3.cloned.1.call-update
  47.7 0.0 all-gather.5.cloned.1.call-start
  47.8 0.0 copy-done.2
  47.8 6.3 %fusion.29 = f32[128,3072]{0,1:T(8,128)S(1)} fusion(bf16[128,1536]{1,0:T(8,128)(2,1)S(1)} %copy-done.2, bf16[1536,3072]{1,0:T(8,128)(2,1)} %param.13), kind=kOutput, calls=%fused_computation.43 | convolution fusion | flops 1207959552 | bytes 11403264 | tf_op jit(solution)/shard_map/dot_general | solution.py:50
  54.1 0.1 slice.76
  54.2 0.9 subtract_convert_fusion.1
  55.1 10.3 %all_gather.10 = bf16[512,64]{0,1:T(8,128)(2,1)S(1)} all-gather(bf16[128,64]{0,1:T(8,128)(2,1)S(1)} %pad_maximum_fusion.1), channel_id=1, replica_groups=mesh['groups'=2,'ctx'=4,'head'=4] {'ctx'}, dimensions={0}, use_global_device_ids=true | all-gather | bytes 81920 | tf_op jit(solution)/shard_map/all_gather | solution.py:65
  65.4 0.1 subtract_convert_fusion
  65.5 0.1 pad_maximum_fusion
  65.5 63.1 %all-gather.3.cloned.1.call-done = bf16[512,4096]{1,0:T(8,128)(2,1)} async-done(((bf16[128,4096]{1,0:T(8,128)(2,1)}), bf16[512,4096]{1,0:T(8,128)(2,1)}) %all-gather.3.cloned.1.call-update) | async-done | bytes 4194320 | tf_op jit(solution)/shard_map/all_gather | solution.py:64
  128.7 16.5 %conditional.1 = (f32[16,128]{1,0:T(8,128)S(1)}, f32[128,16,128]{0,2,1:T(8,128)}) conditional(s32[]{:T(128)} %convert_element_type.31, () %tuple.13, (s32[]{:T(128)}, s32[128]{0:T(128)S(1)}, bf16[128,16,192]{0,2,1:T(8,128)(2,1)S(1)}, bf16[512,4096]{1,0:T(8,128)(2,1)}, bf16[512,64]{0,1:T(8,128)(2,1)S(1)}) %tuple.14), branch_computations={%region_2.0_spmd, %region_3.6_spmd} | conditional | flops 681904256 | bytes 56231472 | solution.py:96
  128.7 0.1 iota_compare_fusion
  128.8 1.3 copy.20
  130.1 6.5 %copy.21 = bf16[512,4096]{0,1:T(8,128)(2,1)} copy(bf16[512,4096]{1,0:T(8,128)(2,1)} %get-tuple-element.29) | data formatting | bytes 8388608 | tf_op jit(solution)/shard_map
  136.6 2.5 %fusion.7 = f32[16,128,512]{2,1,0:T(8,128)S(1)} fusion(bf16[512,16,256]{0,2,1:T(8,128)(2,1)} %bitcast.28, bf16[128,16,192]{2,0,1:T(8,128)(2,1)} %copy.20), kind=kOutput, calls=%fused_computation.8 | convolution fusion | flops 268435456 | bytes 6815744 | tf_op jit(solution)/shard_map/cond/branch_1_fun/thd,nhd->htn/dot_general | solution.py:71
  139.1 0.0 copy-start.1
  139.1 1.2 fusion.28
  140.3 1.0 copy-done.1
  141.3 1.1 fusion.17
  142.4 1.4 fusion.3
  143.9 1.3 copy.26
  145.2 2.2 divide_convert_fusion
  147.3 0.0 all-gather.5.cloned.1.call-update
  147.4 0.2 reduce-scatter.2.cloned.1.call-start
  147.6 44.2 %all-gather.5.cloned.1.call-done = bf16[512,2048]{0,1:T(8,128)(2,1)} async-done(((bf16[128,2048]{0,1:T(8,128)(2,1)}), bf16[512,2048]{0,1:T(8,128)(2,1)}) %all-gather.5.cloned.1.call-update) | async-done | bytes 2097168 | tf_op jit(solution)/shard_map/all_gather | solution.py:101
  191.8 9.0 %convolution_convert_fusion.1 = bf16[512,1792]{1,0:T(8,128)(2,1)} fusion(bf16[512,2048]{0,1:T(8,128)(2,1)} %all-gather.5.cloned.1.call-done, bf16[2048,1792]{1,0:T(8,128)(2,1)} %param.15), kind=kOutput, calls=%fused_computation.24 | convolution fusion | flops 3759013888 | bytes 11272192 | tf_op jit(solution)/shard_map/dot_general | solution.py:100
  200.7 0.0 reduce-scatter.2.cloned.1.call-update
  200.8 30.0 %reduce-scatter.2.cloned.1.call-done = bf16[128,1792]{1,0:T(8,128)(2,1)} async-done(((bf16[512,1792]{1,0:T(8,128)(2,1)}), bf16[128,1792]{1,0:T(8,128)(2,1)}) %reduce-scatter.2.cloned.1.call-update) | async-done | bytes 458768 | tf_op jit(solution)/shard_map/reduce_scatter | solution.py:105
  (7 shorter events, 0.0 us)
Async XLA Ops:
  6.5 1.6 copy-start
  6.5 36.0 %all-reduce.2.cloned.1.call-start = ((), (), s32[]{:S(2)}) async-start(), calls=%async_computation.1 | async-start | bytes 589824 | tf_op jit(solution)/shard_map/psum | solution.py:46
  10.5 37.2 %copy-start.2 = (bf16[128,1536]{1,0:T(8,128)(2,1)S(1)}, bf16[128,1536]{1,0:T(8,128)(2,1)}, u32[]{:S(2)}) copy-start(bf16[128,1536]{1,0:T(8,128)(2,1)} %param.10) | copy-start | bytes 1179652
  10.6 118.1 %all-gather.3.cloned.1.call-start = ((), (), s32[]{:S(2)}) async-start(), calls=%async_computation.2 | async-start | bytes 5242880 | tf_op jit(solution)/shard_map/all_gather | solution.py:64
  47.7 144.0 %all-gather.5.cloned.1.call-start = ((), (), s32[]{:S(2)}) async-start(), calls=%async_computation.3 | async-start | bytes 2621440 | tf_op jit(solution)/shard_map/all_gather | solution.py:101
  139.1 2.2 copy-start.1
  147.4 83.4 %reduce-scatter.2.cloned.1.call-start = ((), (), s32[]{:S(2)}) async-start(), calls=%async_computation.4 | async-start | bytes 2293760 | tf_op jit(solution)/shard_map/reduce_scatter | solution.py:105
Sparse Core Ops, SparseCore 0:
  10.7 31.8 all-reduce.1
  47.9 80.7 all-gather.2
  147.5 44.2 all-gather.4
  200.9 29.8 reduce-scatter.1
where the time goes:
time: 240 us; the launch traced here: 237 us
  waiting for transfers between devices  169 us (70%)
  matrix products  26.6 us (11%)
  between operations  13.2 us (6%)
  local copies, waits for them, and re-layouts  11.8 us (5%)
  blocking collectives  10.3 us (4%)
  other arithmetic  5.8 us (2%)
    all_gather x1, waiting for transfers between devices, body(): keyval = lax.all_gather(keyval_local, 'ctx', axis=0, tiled=True)  63.1 us
    all_gather x1, waiting for transfers between devices, body(): lax.all_gather(attended, 'ctx', axis=0, tiled=True)  44.2 us
    psum x1, waiting for transfers between devices, body(): compressed = lax.psum(partial_sum, 'head')  31.9 us
    reduce_scatter x1, waiting for transfers between devices, body(): lax.psum_scatter(terms.astype(jnp.bfloat16), 'head', scatter_dimension=0,...  30 us
    all_gather x1, blocking collectives, body(): rope_piece = lax.all_gather(rope_key, 'ctx', axis=0, tiled=True)  10.3 us
    dot_general x1, matrix products, body(): jnp.dot(lax.all_gather(attended, 'ctx', axis=0, tiled=True), w_out, prefe...  8.98 us
    another operation x2, local copies, waits for them, and re-layouts  7.84 us
    dot_general x1, matrix products, body(): jnp.dot(q_latent, w_qup, preferred_element_type=jnp.float32)  6.27 us
  transfers between devices with their start and end apart: 4, of which 4 were waited for; matrix products, arithmetic and copies ran while one was open for 3% of the time, Pallas kernels for 0%

commit v1 on v0

v1 whole, which is shorter than its diff:
```python
import math

import jax
import jax.numpy as jnp
from jax import lax
from jax.sharding import PartitionSpec as P

NOPE = 128
ROPE = 64
VDIM = 128
KVRANK = 512


def rotate(pairs, position):
    half = pairs.shape[-1] // 2
    freqs = jnp.exp(
        jnp.arange(half, dtype=jnp.float32) * (-2.0 * math.log(10000.0) / pairs.shape[-1])
    )
    angle = position[..., None] * freqs
    first_half = pairs[..., :half]
    second_half = pairs[..., half:]
    return jnp.concatenate(
        [
            first_half * jnp.cos(angle) - second_half * jnp.sin(angle),
            first_half * jnp.sin(angle) + second_half * jnp.cos(angle),
        ],
        -1,
    )


def finish(compressed, position, latent_gain):
    lat_part = compressed[:, :KVRANK]
    latent = (
        lat_part * lax.rsqrt(jnp.mean(lat_part * lat_part, -1, keepdims=True) + 1e-06) * latent_gain
    ).astype(jnp.bfloat16)
    rope_key = rotate(compressed[:, KVRANK:], position).astype(jnp.bfloat16)
    return (latent, rope_key)


def body(hidden, q_latent, w_down, latent_gain, w_qup, w_kvup, w_out):
    tok_count = q_latent.shape[0]
    first = lax.axis_index("ctx") * tok_count
    position = (first + jnp.arange(tok_count, dtype=jnp.int32)).astype(jnp.float32)
    q_all = lax.all_gather(q_latent, "ctx", axis=0, tiled=True)
    partial_sum = jnp.dot(hidden, w_down, preferred_element_type=jnp.float32)
    compressed = lax.psum(partial_sum, "head")
    latent, rope_key = finish(compressed, position, latent_gain)
    both = lax.all_gather(jnp.concatenate([latent, rope_key], -1), "ctx", axis=0, tiled=True)
    latent, rope_key = both[:, :KVRANK], both[:, KVRANK:]
    width = NOPE + ROPE
    total_tok = both.shape[0]
    heads_here = w_qup.shape[1] // width
    all_index = jnp.arange(total_tok, dtype=jnp.int32)
    query = jnp.dot(q_all, w_qup, preferred_element_type=jnp.float32).reshape(
        total_tok, heads_here, width
    )
    query = jnp.concatenate(
        [query[..., :NOPE], rotate(query[..., NOPE:], all_index.astype(jnp.float32)[:, None])], -1
    ).astype(jnp.bfloat16)
    scale = width ** (-0.5)
    grouped = (
        jnp.dot(latent, w_kvup, preferred_element_type=jnp.float32)
        .astype(jnp.bfloat16)
        .reshape(total_tok, heads_here, NOPE + VDIM)
    )
    keys = jnp.concatenate(
        [
            grouped[..., :NOPE],
            jnp.broadcast_to(rope_key[:, None], (total_tok, heads_here, ROPE)),
        ],
        -1,
    )
    step = min(total_tok, 512)
    pieces = []
    for start in range(0, total_tok, step):
        stop = start + step
        scores = jnp.einsum(
            "thd,nhd->htn", query[start:stop], keys[:stop], preferred_element_type=jnp.float32
        )
        allowed = (all_index[None, :stop] <= all_index[start:stop, None])[None]
        scores = jnp.where(allowed, scores * scale, -1e30)
        probs = jnp.where(allowed, jnp.exp(scores - jnp.max(scores, -1, keepdims=True)), 0.0)
        total = jnp.sum(probs, -1)
        accum = jnp.einsum(
            "htn,nhv->thv",
            probs.astype(jnp.bfloat16),
            grouped[:stop, :, NOPE:],
            preferred_element_type=jnp.float32,
        )
        pieces.append((accum / total.T[..., None]).astype(jnp.bfloat16))
    attended = jnp.concatenate(pieces, 0).reshape(total_tok, heads_here * VDIM)
    terms = jnp.dot(attended, w_out, preferred_element_type=jnp.float32)
    return lax.psum_scatter(terms.astype(jnp.bfloat16), "head", scatter_dimension=0, tiled=True)


def solution(mesh):
    in_specs = (
        P(("groups", "ctx"), "head"),
        P(("groups", "ctx"), None),
        P("head", None),
        P(),
        P(None, "head"),
        P(None, "head"),
        P("head", "ctx"),
    )
    out_specs = P(("groups", "head"), "ctx")
    return jax.shard_map(body, mesh=mesh, in_specs=in_specs, out_specs=out_specs, check_vma=False)
```

time: 240 us -> 168 us (0.70)
  waiting for transfers between devices: 169 us -> 63.3 us
  other arithmetic: 5.8 us -> 21.9 us
  matrix products: 26.6 us -> 40.2 us
  blocking collectives: 10.3 us -> 13 us
    all_gather x2 -> x1, waiting for transfers between devices: 107 us -> 0.01 us  [body(): q_all = lax.all_gather(q_latent, 'ctx', axis=0, tiled=True)]
    sub x0 -> x1, other arithmetic: none -> 17.3 us  [body(): scores - jnp.max(scores, -1, keepdims=True)]
    dot_general x5 -> x4, matrix products: 20 us -> 31.1 us  [the longest x1 9.22 us: body(): jnp.einsum('thd,nhd->htn', query[start:stop], keys[:stop], preferred_elem...]
    another operation x2 -> x0, local copies, waits for them, and re-layouts: 7.84 us -> none
    reshape x0 -> x1, local copies, waits for them, and re-layouts: none -> 6.47 us  [body(): grouped = jnp.dot(latent, w_kvup, preferred_element_type=jnp.float32).ast...]
    slice x0 -> x3, local copies, waits for them, and re-layouts: none -> 3.12 us  [the longest x1 3.12 us: body(): grouped[..., :NOPE]]
    all_gather x1, blocking collectives: 10.3 us -> 13 us  [body(): lax.all_gather(jnp.concatenate([latent, rope_key], -1), 'ctx', axis=0, ti...]
    dot_general x1, matrix products: 4.1 us -> 6.7 us  [body(): jnp.dot(latent, w_kvup, preferred_element_type=jnp.float32)]
  transfers between devices with their start and end apart: 4 -> 3, of which waited for: 4 -> 2; matrix products, arithmetic and copies ran while one was open for 3% -> 12% of each run, Pallas kernels for 0% -> 0%
where the time goes in v1:
time: 168 us; the launch traced here: 165 us
  waiting for transfers between devices  63.3 us (38%)
  matrix products  40.2 us (24%)
  other arithmetic  21.9 us (13%)
  between operations  15 us (9%)
  blocking collectives  13 us (8%)
  local copies, waits for them, and re-layouts  11.6 us (7%)
    reduce_scatter x1, waiting for transfers between devices, body(): lax.psum_scatter(terms.astype(jnp.bfloat16), 'head', scatter_dimension=0,...  31.9 us
    psum x1, waiting for transfers between devices, body(): compressed = lax.psum(partial_sum, 'head')  30.8 us
    sub x1, other arithmetic, body(): scores - jnp.max(scores, -1, keepdims=True)  17.3 us
    all_gather x1, blocking collectives, body(): lax.all_gather(jnp.concatenate([latent, rope_key], -1), 'ctx', axis=0, ti...  13 us
    dot_general x1, matrix products, body(): jnp.einsum('thd,nhd->htn', query[start:stop], keys[:stop], preferred_elem...  9.22 us
    dot_general x1, matrix products, body(): terms = jnp.dot(attended, w_out, preferred_element_type=jnp.float32)  8.42 us
    dot_general x1, matrix products, body(): jnp.dot(q_all, w_qup, preferred_element_type=jnp.float32)  8.18 us
    dot_general x1, matrix products, body(): jnp.dot(latent, w_kvup, preferred_element_type=jnp.float32)  6.7 us
  transfers between devices with their start and end apart: 3, of which 2 were waited for; matrix products, arithmetic and copies ran while one was open for 12% of the time, Pallas kernels for 0%

profile of v1, /device:TPU:11, one launch (start us, length us, event | category | flops | bytes accessed | tf_op | source)
XLA Modules:
  0.0 165.2 jit_solution(6852648006071574328)
XLA Ops:
  7.4 0.0 copy-start
  7.4 0.0 copy-start.4
  7.4 0.0 all-reduce.2.cloned.1.call-start
  7.4 1.6 copy-done
  8.9 2.4 %fusion.33 = f32[128,576]{0,1:T(8,128)} fusion(bf16[128,1792]{1,0:T(8,128)(2,1)} %param.7, bf16[1792,576]{0,1:T(8,128)(2,1)S(1)} %copy-done), kind=kOutput, calls=%fused_computation.51 | convolution fusion | flops 264241152 | bytes 2818048 | tf_op jit(solution)/shard_map/dot_general | solution.py:45
  11.4 0.0 all-reduce.2.cloned.1.call-update
  11.4 0.0 all-gather.2.cloned.1.call-start
  11.4 0.5 all-gather.2.cloned.1.call-update
  12.0 0.0 reduce-scatter.2.cloned.1.call-start
  12.1 0.1 iota_compare_fusion
  12.2 0.3 multiply_cosine_fusion
  12.5 30.8 %all-reduce.2.cloned.1.call-done = f32[128,576]{0,1:T(8,128)} async-done(((f32[128,576]{0,1:T(8,128)}), f32[128,576]{0,1:T(8,128)}) %all-reduce.2.cloned.1.call-update) | async-done | bytes 294928 | tf_op jit(solution)/shard_map/psum | solution.py:46
  43.3 1.0 multiply_reduce_fusion
  44.3 0.9 fusion.26
  45.2 0.0 copy-done.4
  45.2 1.1 multiply_convert_fusion
  46.3 13.0 %all_gather.6 = bf16[512,576]{0,1:T(8,128)(2,1)S(1)} all-gather(bf16[128,576]{0,1:T(8,128)(2,1)S(1)} %pad_maximum_fusion), channel_id=1, replica_groups=mesh['groups'=2,'ctx'=4,'head'=4] {'ctx'}, dimensions={0}, use_global_device_ids=true | all-gather | bytes 737280 | tf_op jit(solution)/shard_map/all_gather | solution.py:48
  59.3 0.0 copy-start.3
  59.3 6.7 %convolution_convert_fusion = bf16[512,4096]{1,0:T(8,128)(2,1)} fusion(bf16[512,4096]{1,0:T(8,128)(2,1)} %param.12, bf16[512,576]{0,1:T(8,128)(2,1)S(1)} %all_gather.6), kind=kOutput, calls=%fused_computation.9 | convolution fusion | flops 2149580800 | bytes 8912896 | tf_op jit(solution)/shard_map/dot_general | solution.py:62
  66.1 0.0 copy-done.3
  66.1 6.5 %copy.20 = bf16[512,4096]{0,1:T(8,128)(2,1)} copy(bf16[512,4096]{1,0:T(8,128)(2,1)} %convolution_convert_fusion) | data formatting | bytes 8388608 | tf_op jit(solution)/shard_map/reshape | solution.py:64
  72.5 3.1 %slice.55 = bf16[512,16,128]{0,2,1:T(8,128)(2,1)} slice(bf16[512,16,256]{0,2,1:T(8,128)(2,1)} %bitcast.16), slice={[0:512], [0:16], [0:128]} | slice | bytes 4194304 | tf_op jit(solution)/shard_map/slice | solution.py:68
  75.6 0.0 all-gather.2.cloned.1.call-done
  75.6 8.2 %fusion.34 = f32[512,3072]{0,1:T(8,128)S(1)} fusion(bf16[512,1536]{1,0:T(8,128)(2,1)} %all-gather.2.cloned.1.call-done, bf16[1536,3072]{1,0:T(8,128)(2,1)} %param.11), kind=kOutput, calls=%fused_computation.52 | convolution fusion | flops 4831838208 | bytes 17301504 | tf_op jit(solution)/shard_map/dot_general | solution.py:54
  83.8 0.0 slice-start
  83.8 0.0 copy-start.2
  83.9 0.3 slice.72
  84.2 1.1 subtract_convert_fusion
  85.3 0.0 slice-done
  85.3 0.1 broadcast_in_dim.37
  85.4 0.1 copy-done.2
  85.5 9.2 %fusion.8 = f32[16,512,512]{1,2,0:T(8,128)} fusion(bf16[512,16,32]{0,2,1:T(8,128)(2,1)} %get-tuple-element.6, bf16[512,16,32]{0,2,1:T(8,128)(2,1)S(1)} %get-tuple-element.5, bf16[512,16,128]{0,2,1:T(8,128)(2,1)S(1)} %slice.72, bf16[512,16,64]{0,2,1:T(8,128)(2,1)S(1)} %broadcast_in_dim.37, bf16[512,16,128]{0,2,1:T(8,128)(2,1)S(1)} %copy-done.2), kind=kOutput, calls=%fused_computation.13 | convolution fusion | flops 1626341376 | bytes 23068672 | tf_op jit(solution)/shard_map/thd,nhd->htn/dot_general | solution.py:77
  94.7 17.3 %fusion.32 = (f32[16,512]{1,0:T(8,128)S(1)}, bf16[16,512,512]{1,2,0:T(8,128)(2,1)}) fusion(f32[16,512,512]{1,2,0:T(8,128)} %fusion.8, pred[512,512]{0,1:T(8,128)(4,1)S(1)} %iota_compare_fusion), kind=kOutput, calls=%fused_computation.50 | output fusion | flops 33554944 | bytes 25460736 | tf_op jit(solution)/shard_map/sub | solution.py:82
  112.0 5.3 %fusion.7 = bf16[512,16,128]{0,2,1:T(8,128)(2,1)S(1)} fusion(bf16[16,512,512]{1,2,0:T(8,128)(2,1)} %get-tuple-element.12, bf16[512,16,256]{0,2,1:T(8,128)(2,1)} %bitcast.17, f32[512,16]{0,1:T(8,128)S(1)} %bitcast.21), kind=kOutput, calls=%fused_computation.12 | convolution fusion | flops 1075838976 | bytes 12615680 | tf_op jit(solution)/shard_map/htn,nhv->thv/dot_general | solution.py:84
  117.3 0.0 copy-start.1
  117.3 8.4 %convolution_convert_fusion.1 = bf16[512,1792]{1,0:T(8,128)(2,1)} fusion(bf16[512,2048]{0,1:T(8,128)(2,1)S(1)} %bitcast.20, bf16[2048,1792]{1,0:T(8,128)(2,1)} %param.13), kind=kOutput, calls=%fused_computation.22 | convolution fusion | flops 3759013888 | bytes 11272192 | tf_op jit(solution)/shard_map/dot_general | solution.py:92
  125.7 0.0 reduce-scatter.2.cloned.1.call-update
  125.8 31.9 %reduce-scatter.2.cloned.1.call-done = bf16[128,1792]{1,0:T(8,128)(2,1)} async-done(((bf16[512,1792]{1,0:T(8,128)(2,1)}), bf16[128,1792]{1,0:T(8,128)(2,1)}) %reduce-scatter.2.cloned.1.call-update) | async-done | bytes 458768 | tf_op jit(solution)/shard_map/reduce_scatter | solution.py:93
  157.7 0.0 copy-done.1
  (5 shorter events, 0.0 us)
Async XLA Ops:
  7.4 1.6 copy-start
  7.4 37.8 %copy-start.4 = (f32[512]{0:T(512)S(1)}, f32[512]{0:T(512)}, u32[]{:S(2)}) copy-start(f32[512]{0:T(512)} %param.10) | copy-start | bytes 6148
  7.4 35.9 %all-reduce.2.cloned.1.call-start = ((), (), s32[]{:S(2)}) async-start(), calls=%async_computation.1 | async-start | bytes 589824 | tf_op jit(solution)/shard_map/psum | solution.py:46
  11.4 64.2 %all-gather.2.cloned.1.call-start = ((), (), s32[]{:S(2)}) async-start(), calls=%async_computation.2 | async-start | bytes 1966080 | tf_op jit(solution)/shard_map/all_gather | solution.py:44
  12.0 145.7 %reduce-scatter.2.cloned.1.call-start = ((), (), s32[]{:S(2)}) async-start(), calls=%async_computation.3 | async-start | bytes 2293760 | tf_op jit(solution)/shard_map/reduce_scatter | solution.py:93
  59.3 6.7 %copy-start.3 = (bf16[512,576]{0,1:T(8,128)(2,1)}, bf16[512,576]{0,1:T(8,128)(2,1)S(1)}, u32[]{:S(2)}) copy-start(bf16[512,576]{0,1:T(8,128)(2,1)S(1)} %all_gather.6) | copy-start | bytes 1769476
  83.8 1.5 slice-start
  83.8 1.6 copy-start.2
  117.3 40.4 %copy-start.1 = (bf16[1792,576]{0,1:T(8,128)(2,1)S(1)}, bf16[1792,576]{0,1:T(8,128)(2,1)}, u32[]{:S(2)}) copy-start(bf16[1792,576]{0,1:T(8,128)(2,1)} %param.9) | copy-start | bytes 6193156
Sparse Core Ops, SparseCore 0:
  11.5 31.7 all-reduce.1
  125.9 31.7 reduce-scatter.1
Sparse Core Ops, SparseCore 1:
  13.4 36.7 all-gather.1

commit v2 on v1

v2 whole, which is shorter than its diff:
```python
import functools
import math

import jax
import jax.numpy as jnp
import numpy as np
from jax import lax
from jax.experimental import pallas as pl
from jax.experimental.pallas import tpu as pltpu
from jax.sharding import PartitionSpec as P

NOPE = 128
ROPE = 64
VDIM = 128
KVRANK = 512
MESH = pl.DeviceIdType.MESH
F32 = jnp.float32
BF16 = jnp.bfloat16


def tables(count):
    half = ROPE // 2
    freqs = np.exp(np.arange(half, dtype=np.float32) * np.float32(-2.0 * math.log(10000.0) / ROPE))
    angle = np.arange(count, dtype=np.float32)[:, None] * freqs.astype(np.float32)[None]
    cos = np.cos(angle.astype(np.float64)).astype(np.float32)
    sin = np.sin(angle.astype(np.float64)).astype(np.float32)
    one, zero = np.ones((count, 64), np.float32), np.zeros((count, 64), np.float32)
    return (
        np.concatenate([cos, cos, one, one, cos, cos], 1),
        np.concatenate([-sin, sin, zero, zero, -sin, sin], 1),
    )


def kernel(
    C, H, hid, ql, wd, gain, wq, wkv, wo, cos_h, sin_h, out,
    hid_v, wd_v, wq_v, wkv_v, wo_v, cos_v, sin_v, qlat, part, rs, lat, q_s, kk, vv, att,
    terms, precv, xs, xr, load_sem, q_sem, lat_sem, rs_sem, p_sem, x_sem, send_sem,
):
    X = H // 2
    c, h = lax.axis_index("ctx"), lax.axis_index("head")
    core = lax.rem(h, 2)
    chip = lax.div(h, 2)
    mate = h + 1 - 2 * core
    tok = ql.shape[0]
    sub = tok // H
    T = C * tok
    pairs = q_s.shape[0]
    sends = []

    def load(i, src, dst):
        copy = pltpu.make_async_copy(src, dst, load_sem.at[i])
        copy.start()
        return copy

    own_q = load(0, ql, qlat.at[pl.ds(0, tok)])
    load_hid = load(1, hid, hid_v)
    load_wd = load(2, wd, wd_v)
    load_cos = load(3, cos_h, cos_v)
    load_sin = load(4, sin_h, sin_v)
    load_wq = load(5, wq, wq_v)
    load_wkv = load(6, wkv, wkv_v)
    load_wo = load(7, wo, wo_v)

    barrier = pltpu.get_barrier_semaphore()
    for d in range(1, C):
        pl.semaphore_signal(
            barrier, inc=1, device_id={"ctx": lax.rem(c + d, C)}, device_id_type=MESH
        )
    for e in range(1, H):
        pl.semaphore_signal(
            barrier, inc=1, device_id={"head": lax.rem(h + e, H)}, device_id_type=MESH
        )

    def remote(src, dst, sem, device):
        copy = pltpu.make_async_remote_copy(
            src_ref=src,
            dst_ref=dst,
            send_sem=send_sem.at[len(sends)],
            recv_sem=sem,
            device_id=device,
            device_id_type=MESH,
        )
        copy.start()
        sends.append(copy)

    def arrived(dst, sem):
        pltpu.make_async_copy(dst, dst, sem).wait()

    def rows(slot, hh):
        return pl.ds(pl.multiple_of(slot * tok + hh * sub, sub), sub)

    own_q.wait()
    pl.semaphore_wait(barrier, C - 1 + H - 1)
    for d in range(1, C):
        remote(
            qlat.at[rows(0, h)],
            qlat.at[rows(C - d, h)],
            q_sem.at[(C - d) * H + h],
            {"ctx": lax.rem(c + d, C)},
        )

    load_hid.wait()
    load_wd.wait()
    part[...] = jnp.dot(hid_v[...], wd_v[...], preferred_element_type=F32).reshape(part.shape)
    for e in range(1, H):
        to = lax.rem(h + e, H)
        remote(part.at[to], rs.at[e], rs_sem.at[e], {"head": to})

    lane = lax.broadcasted_iota(jnp.int32, (1, 128), 1)
    first = lax.rem(lane, 64) < 32
    low = lane < 64

    def project(slot, count):
        def group(jj, _):
            f = jnp.dot(
                qlat[slot * tok : (slot + count) * tok, :],
                wq_v[:, pl.ds(pl.multiple_of(jj * 768, 768), 768)],
                preferred_element_type=F32,
            )
            for s in range(count):
                true = pl.ds(pl.multiple_of(lax.rem(c + slot + s, C) * tok, tok), tok)
                for p in range(2):
                    piece = f[s * tok : (s + 1) * tok, p * 384 : (p + 1) * 384]
                    q_s[2 * jj + p, true, 0:128] = piece[:, :128].astype(BF16)
                    for w in range(2):
                        v = piece[:, 128 * (w + 1) : 128 * (w + 2)]
                        swapped = jnp.where(first, pltpu.roll(v, 96, 1), pltpu.roll(v, 32, 1))
                        side = slice(128 * w, 128 * (w + 1))
                        v = v * cos_v[true, side] + swapped * sin_v[true, side]
                        q_s[2 * jj + p, true, 128 * (w + 1) : 128 * (w + 2)] = v.astype(BF16)
            return 0

        lax.fori_loop(0, pairs // 2, group, 0)

    load_cos.wait()
    load_sin.wait()
    load_wq.wait()
    project(0, 1)

    for e in range(1, H):
        arrived(rs.at[e], rs_sem.at[e])
    total = part[h]
    for e in range(1, H):
        total = total + rs[e]
    lp = total[:, :KVRANK]
    latent = lp * lax.rsqrt(jnp.mean(lp * lp, -1, keepdims=True) + 1e-06) * gain[...]
    here = pl.ds(pl.multiple_of(c * tok + h * sub, sub), sub)
    a = total[:, KVRANK : KVRANK + 32]
    b = total[:, KVRANK + 32 : KVRANK + 64]
    cs, sn = cos_v[here, 0:32], sin_v[here, 32:64]
    ra, rb = a * cs - b * sn, a * sn + b * cs
    lat[here, 0:KVRANK] = latent.astype(BF16)
    lat[here, KVRANK:] = jnp.concatenate([ra, rb, ra, rb], -1).astype(BF16)

    def share_lat(cc, hh, device):
        r = rows(cc, hh)
        remote(lat.at[r], lat.at[r], lat_sem.at[cc * H + hh], device)

    def share_q(slot, hh, device):
        r = rows(slot, hh)
        remote(qlat.at[r], qlat.at[r], q_sem.at[slot * H + hh], device)

    def across(e):
        return lax.rem(h + 2 * e, H)

    for d in range(1, C):
        share_lat(c, h, {"ctx": lax.rem(c + d, C)})
    for e in range(1, X):
        share_lat(c, h, {"head": across(e)})
    share_lat(c, h, {"head": mate})

    for s in list(range(1, C)):
        arrived(qlat.at[rows(s, h)], q_sem.at[s * H + h])
        for e in range(1, X):
            share_q(s, h, {"head": across(e)})
        share_q(s, h, {"head": mate})
    for d in range(1, C):
        cc = lax.rem(c + d, C)
        arrived(lat.at[rows(cc, h)], lat_sem.at[cc * H + h])
        for e in range(1, X):
            share_lat(cc, h, {"head": across(e)})
        share_lat(cc, h, {"head": mate})
    for s in range(1, C):
        for e in range(1, X):
            hh = across(e)
            arrived(qlat.at[rows(s, hh)], q_sem.at[s * H + hh])
            share_q(s, hh, {"head": mate})
    for d in range(C):
        cc = lax.rem(c + d, C)
        for e in range(1, X):
            hh = across(e)
            arrived(lat.at[rows(cc, hh)], lat_sem.at[cc * H + hh])
            share_lat(cc, hh, {"head": mate})
    for s in range(1, C):
        for e in range(X):
            hh = lax.rem(mate + 2 * e, H)
            arrived(qlat.at[rows(s, hh)], q_sem.at[s * H + hh])
    step = max(n for n in (1, 2, 3) if (C - 1) % n == 0)
    for s in range(1, C, step):
        project(s, step)
    for d in range(C):
        cc = lax.rem(c + d, C)
        for e in range(X):
            hh = lax.rem(mate + 2 * e, H)
            arrived(lat.at[rows(cc, hh)], lat_sem.at[cc * H + hh])

    load_wkv.wait()
    span = min(T, 512)

    def keyval(j, _):
        for r0 in range(0, T, span):
            r = slice(r0, r0 + span)
            f = jnp.dot(
                lat[r, 0:KVRANK],
                wkv_v[:, pl.ds(pl.multiple_of(j * 512, 512), 512)],
                preferred_element_type=F32,
            )
            rk = lat[r, KVRANK:].astype(F32)
            kk[2 * j, r, 0:128] = f[:, 0:128].astype(BF16)
            kk[2 * j, r, 128:256] = jnp.where(low, rk, 0.0).astype(BF16)
            vv[2 * j, r, :] = f[:, 128:256].astype(BF16)
            k1 = pltpu.roll(f[:, 256:384], 64, 1)
            kk[2 * j + 1, r, 0:128] = jnp.where(low, 0.0, k1).astype(BF16)
            kk[2 * j + 1, r, 128:256] = jnp.where(low, k1, rk).astype(BF16)
            vv[2 * j + 1, r, :] = f[:, 384:512].astype(BF16)
        return 0

    lax.fori_loop(0, pairs, keyval, 0)

    R = T // X
    small = min(R, 256)
    factor = (NOPE + ROPE) ** (-0.5) * math.log2(math.e)

    def attend(bb):
        for r0 in range(0, R, small):
            start = bb * R + r0
            nk = start + small
            allowed = lax.broadcasted_iota(jnp.int32, (small, nk), 1) <= (
                lax.broadcasted_iota(jnp.int32, (small, nk), 0) + start
            )

            def pair(j, _):
                for i in range(2):
                    s = lax.dot_general(
                        q_s[j, start:nk, 128 * i : 128 * i + 256],
                        kk[2 * j + i, 0:nk, :],
                        (((1,), (1,)), ((), ())),
                        preferred_element_type=F32,
                    )
                    s = jnp.where(allowed, s, -1e30)
                    p = jnp.exp2((s - jnp.max(s, -1, keepdims=True)) * factor)
                    o = jnp.dot(p.astype(BF16), vv[2 * j + i, 0:nk, :], preferred_element_type=F32)
                    o = o / jnp.sum(p, -1, keepdims=True)
                    at = pl.ds(pl.multiple_of(j * 256 + i * 128, 128), 128)
                    att[r0 : r0 + small, at] = o.astype(BF16)
                return 0

            lax.fori_loop(0, pairs, pair, 0)

    chunks, _, sub2, nc = precv.shape[1:2] + (0,) + precv.shape[2:]

    def finish(t, n):
        arrived(precv.at[t, n], p_sem.at[t * chunks + n])
        value = terms[t, n, core].astype(F32) + precv[t, n].astype(F32)
        if t < X - 1:
            xs[t, n] = value.astype(BF16)
            remote(
                xs.at[t, n],
                xr.at[t, n],
                x_sem.at[t * chunks + n],
                {"head": lax.rem(h + 2 * (1 + t), H)},
            )
            return
        for u in range(X - 1):
            arrived(xr.at[u, n], x_sem.at[u * chunks + n])
            value = value + xr[u, n].astype(F32)
        out[:, n * nc : (n + 1) * nc] = value.astype(BF16)

    for t in range(X):
        block = lax.rem(chip + 1 + t, X)
        for bb in range(X):
            pl.when(block == bb)(functools.partial(attend, bb))
        if t == 0:
            load_wo.wait()
        for n in range(chunks):
            f = jnp.dot(att[...], wo_v[:, n * nc : (n + 1) * nc], preferred_element_type=F32)
            terms[t, n] = f.astype(BF16).reshape(2, sub2, nc)
            remote(
                terms.at[t, n, 1 - core], precv.at[t, n], p_sem.at[t * chunks + n], {"head": mate}
            )
            if n:
                finish(t, n - 1)
        finish(t, chunks - 1)
    for copy in sends:
        copy.wait_send()


def body(C, H, hidden, q_latent, w_down, latent_gain, w_qup, w_kvup, w_out):
    tok, rank = q_latent.shape
    T, X = C * tok, H // 2
    heads = w_qup.shape[1] // (NOPE + ROPE)
    cols = w_out.shape[1]
    nc = 256 if cols % 256 == 0 else cols
    chunks = cols // nc
    sub, sub2 = tok // H, T // H
    cos, sin = tables(T)
    wide = KVRANK + ROPE
    n_send = (C - 1) * (2 + X - 1 + X) + C * (X - 1 + X) + H - 1 + X * chunks + (X - 1) * chunks
    dma = pltpu.SemaphoreType.DMA
    hbm = pl.BlockSpec(memory_space=pl.ANY)
    vmem = pl.BlockSpec(memory_space=pltpu.VMEM)
    return pl.pallas_call(
        functools.partial(kernel, C, H),
        out_shape=jax.ShapeDtypeStruct((sub2, cols), BF16),
        in_specs=[hbm, hbm, hbm, vmem, hbm, hbm, hbm, hbm, hbm],
        out_specs=vmem,
        scratch_shapes=[
            pltpu.VMEM(hidden.shape, BF16),
            pltpu.VMEM(w_down.shape, BF16),
            pltpu.VMEM(w_qup.shape, BF16),
            pltpu.VMEM(w_kvup.shape, BF16),
            pltpu.VMEM(w_out.shape, BF16),
            pltpu.VMEM((T, 256), F32),
            pltpu.VMEM((T, 256), F32),
            pltpu.VMEM((T, rank), BF16),
            pltpu.VMEM((H, sub, wide), F32),
            pltpu.VMEM((H, sub, wide), F32),
            pltpu.VMEM((T, KVRANK + 128), BF16),
            pltpu.VMEM((heads // 2, T, 384), BF16),
            pltpu.VMEM((heads, T, 256), BF16),
            pltpu.VMEM((heads, T, VDIM), BF16),
            pltpu.VMEM((T // X, heads * VDIM), BF16),
            pltpu.VMEM((X, chunks, 2, sub2, nc), BF16),
            pltpu.VMEM((X, chunks, sub2, nc), BF16),
            pltpu.VMEM((X - 1, chunks, sub2, nc), BF16),
            pltpu.VMEM((X - 1, chunks, sub2, nc), BF16),
            dma((8,)),
            dma((C * H,)),
            dma((C * H,)),
            dma((H,)),
            dma((X * chunks,)),
            dma((X * chunks,)),
            dma((n_send,)),
        ],
        compiler_params=pltpu.CompilerParams(
            collective_id=0, has_side_effects=True, vmem_limit_bytes=60 * 1024 * 1024
        ),
    )(
        hidden, q_latent, w_down, latent_gain.reshape(1, -1), w_qup, w_kvup, w_out,
        jnp.asarray(cos), jnp.asarray(sin),
    )


def solution(mesh):
    in_specs = (
        P(("groups", "ctx"), "head"),
        P(("groups", "ctx"), None),
        P("head", None),
        P(),
        P(None, "head"),
        P(None, "head"),
        P("head", "ctx"),
    )
    out_specs = P(("groups", "head"), "ctx")
    return jax.shard_map(
        functools.partial(body, mesh.shape["ctx"], mesh.shape["head"]),
        mesh=mesh,
        in_specs=in_specs,
        out_specs=out_specs,
        check_vma=False,
    )
```

time: 168 us -> 68.3 us (0.41); the launches traced: 165 us -> 68.1 us
  waiting for transfers between devices: 63.3 us -> 0 us
  Pallas kernels: 0 us -> 62.2 us
  matrix products: 40.2 us -> 0 us
  other arithmetic: 21.9 us -> 0 us
  between operations: 15 us -> 0.01 us
  blocking collectives: 13 us -> 0 us
  local copies, waits for them, and re-layouts: 11.6 us -> 5.91 us
    pallas_call x0 -> x1, Pallas kernels: none -> 62.2 us  [body(): pl.pallas_call(functools.partial(kernel, C, H), out_shape=jax.ShapeDtypeS...]
    dot_general x6 -> x0, matrix products: 40.2 us -> none  [the longest x1 9.22 us: body(): jnp.einsum('thd,nhd->htn', query[start:stop], keys[:stop], preferred_elem...]
    reduce_scatter x1 -> x0, waiting for transfers between devices: 31.9 us -> none  [body(): lax.psum_scatter(terms.astype(jnp.bfloat16), 'head', scatter_dimension=0,...]
    psum x1 -> x0, waiting for transfers between devices: 30.8 us -> none  [body(): compressed = lax.psum(partial_sum, 'head')]
    sub x1 -> x0, other arithmetic: 17.3 us -> none  [body(): scores - jnp.max(scores, -1, keepdims=True)]
    all_gather x1 -> x0, blocking collectives: 13 us -> none  [body(): lax.all_gather(jnp.concatenate([latent, rope_key], -1), 'ctx', axis=0, ti...]
    reshape x1 -> x0, local copies, waits for them, and re-layouts: 6.47 us -> none  [body(): grouped = jnp.dot(latent, w_kvup, preferred_element_type=jnp.float32).ast...]
    unnamed x10 -> x2, local copies, waits for them, and re-layouts: 1.65 us -> 5.91 us
  transfers between devices with their start and end apart: 3 -> 0, of which waited for: 2 -> 0; matrix products, arithmetic and copies ran while one was open for 12% -> 0% of each run, Pallas kernels for 0% -> 0%
where the time goes in v2:
time: 68.3 us; the launch traced here: 68.1 us
  Pallas kernels  62.2 us (91%)
  local copies, waits for them, and re-layouts  5.91 us (9%)
    pallas_call x1, Pallas kernels, body(): pl.pallas_call(functools.partial(kernel, C, H), out_shape=jax.ShapeDtypeS...  62.2 us
    unnamed x2, local copies, waits for them, and re-layouts  5.91 us

profile of v2, /device:TPU:11, one launch (start us, length us, event | category | flops | bytes accessed | tf_op | source)
XLA Modules:
  0.0 68.1 jit_solution(6227574129631966069)
XLA Ops:
  0.0 4.1 %copy.10.wd = bf16[1792,576]{1,0:T(8,128)(2,1)} copy(bf16[1792,576]{0,1:T(8,128)(2,1)} %param.11) | data formatting | bytes 4128768 | tf_op args[2]
  4.1 62.2 %shard_map.91 = bf16[128,1792]{1,0:T(8,128)(2,1)} custom-call(bf16[128,1792]{1,0:T(8,128)(2,1)} %hid.1, bf16[128,1536]{1,0:T(8,128)(2,1)} %ql.1, bf16[1792,576]{1,0:T(8,128)(2,1)} %copy.10.wd, f32[1,512]{1,0:T(1,128)} %bitcast.1, bf16[1536,3072]{1,0:T(8,128)(2,1)} %wq.1, bf16[512,4096]{1,0:T(8,128)(2,1)} %wkv.1, bf16[2048,1792]{1,0:T(8,128)(2,1)} %wo.1, ...), custom_call_target="tpu_custom_call" | custom-call | tf_op jit(solution)/shard_map/pallas_call | solution.py:312
  66.3 1.8 %copy.12 = bf16[128,1792]{1,0:T(8,128)(2,1)} copy(bf16[128,1792]{1,0:T(8,128)(2,1)} %shard_map.91) | data formatting | bytes 917504

commit v3 on v2

--- a/solution.py
+++ b/solution.py
@@ -55,12 +55,6 @@
     own_q = load(0, ql, qlat.at[pl.ds(0, tok)])
     load_hid = load(1, hid, hid_v)
     load_wd = load(2, wd, wd_v)
-    load_cos = load(3, cos_h, cos_v)
-    load_sin = load(4, sin_h, sin_v)
-    load_wq = load(5, wq, wq_v)
-    load_wkv = load(6, wkv, wkv_v)
-    load_wo = load(7, wo, wo_v)
-
     barrier = pltpu.get_barrier_semaphore()
     for d in range(1, C):
         pl.semaphore_signal(
@@ -101,7 +95,14 @@
 
     load_hid.wait()
     load_wd.wait()
-    part[...] = jnp.dot(hid_v[...], wd_v[...], preferred_element_type=F32).reshape(part.shape)
+    load_cos = load(3, cos_h, cos_v)
+    load_sin = load(4, sin_h, sin_v)
+    load_wq = load(5, wq, wq_v)
+    load_wkv = load(6, wkv, wkv_v)
+    load_wo = load(7, wo, wo_v)
+    part[...] = lax.dot_general(
+        hid_v[...], wd_v[...], (((1,), (1,)), ((), ())), preferred_element_type=F32
+    ).reshape(part.shape)
     for e in range(1, H):
         to = lax.rem(h + e, H)
         remote(part.at[to], rs.at[e], rs_sem.at[e], {"head": to})
@@ -169,7 +170,7 @@
         share_lat(c, h, {"head": across(e)})
     share_lat(c, h, {"head": mate})
 
-    for s in list(range(1, C)):
+    for s in range(1, C):
         arrived(qlat.at[rows(s, h)], q_sem.at[s * H + h])
         for e in range(1, X):
             share_q(s, h, {"head": across(e)})
@@ -235,27 +236,38 @@
         for r0 in range(0, R, small):
             start = bb * R + r0
             nk = start + small
-            allowed = lax.broadcasted_iota(jnp.int32, (small, nk), 1) <= (
-                lax.broadcasted_iota(jnp.int32, (small, nk), 0) + start
-            )
+            allowed = lax.broadcasted_iota(jnp.int32, (small, small), 1) <= (
+                lax.broadcasted_iota(jnp.int32, (small, small), 0)
+            )
+            cuts = [(0, start), (start, nk)] if start else [(0, nk)]
 
             def pair(j, _):
                 for i in range(2):
-                    s = lax.dot_general(
-                        q_s[j, start:nk, 128 * i : 128 * i + 256],
-                        kk[2 * j + i, 0:nk, :],
-                        (((1,), (1,)), ((), ())),
-                        preferred_element_type=F32,
+                    q = q_s[j, start:nk, 128 * i : 128 * i + 256]
+                    s = [
+                        lax.dot_general(
+                            q,
+                            kk[2 * j + i, lo:hi, :],
+                            (((1,), (1,)), ((), ())),
+                            preferred_element_type=F32,
+                        )
+                        for lo, hi in cuts
+                    ]
+                    s[-1] = jnp.where(allowed, s[-1], -1e30)
+                    most = functools.reduce(jnp.maximum, [jnp.max(v, -1, keepdims=True) for v in s])
+                    p = [jnp.exp2((v - most) * factor) for v in s]
+                    total = sum(jnp.sum(v, -1, keepdims=True) for v in p)
+                    o = sum(
+                        jnp.dot(
+                            v.astype(BF16), vv[2 * j + i, lo:hi, :], preferred_element_type=F32
+                        )
+                        for v, (lo, hi) in zip(p, cuts)
                     )
-                    s = jnp.where(allowed, s, -1e30)
-                    p = jnp.exp2((s - jnp.max(s, -1, keepdims=True)) * factor)
-                    o = jnp.dot(p.astype(BF16), vv[2 * j + i, 0:nk, :], preferred_element_type=F32)
-                    o = o / jnp.sum(p, -1, keepdims=True)
                     at = pl.ds(pl.multiple_of(j * 256 + i * 128, 128), 128)
-                    att[r0 : r0 + small, at] = o.astype(BF16)
+                    att[r0 : r0 + small, at] = (o / total).astype(BF16)
                 return 0
 
-            lax.fori_loop(0, pairs, pair, 0)
+            lax.fori_loop(0, pairs, pair, 0, unroll=2 if T <= 512 else 1)
 
     chunks, _, sub2, nc = precv.shape[1:2] + (0,) + precv.shape[2:]
 
@@ -316,7 +328,7 @@
         out_specs=vmem,
         scratch_shapes=[
             pltpu.VMEM(hidden.shape, BF16),
-            pltpu.VMEM(w_down.shape, BF16),
+            pltpu.VMEM(w_down.shape[::-1], BF16),
             pltpu.VMEM(w_qup.shape, BF16),
             pltpu.VMEM(w_kvup.shape, BF16),
             pltpu.VMEM(w_out.shape, BF16),
@@ -346,7 +358,7 @@
             collective_id=0, has_side_effects=True, vmem_limit_bytes=60 * 1024 * 1024
         ),
     )(
-        hidden, q_latent, w_down, latent_gain.reshape(1, -1), w_qup, w_kvup, w_out,
+        hidden, q_latent, w_down.T, latent_gain.reshape(1, -1), w_qup, w_kvup, w_out,
         jnp.asarray(cos), jnp.asarray(sin),
     )
 

time: 68.3 us -> 60.2 us (0.88); the launches traced: 68.1 us -> 59.1 us
  Pallas kernels: 62.2 us -> 57.3 us
  local copies, waits for them, and re-layouts: 5.91 us -> 1.82 us
    pallas_call x1, Pallas kernels: 62.2 us -> 57.3 us  [body(): pl.pallas_call(functools.partial(kernel, C, H), out_shape=jax.ShapeDtypeS...]
    unnamed x2 -> x1, local copies, waits for them, and re-layouts: 5.91 us -> 1.82 us
where the time goes in v3:
time: 60.2 us; the launch traced here: 59.1 us
  Pallas kernels  57.3 us (95%)
  local copies, waits for them, and re-layouts  1.82 us (3%)
    pallas_call x1, Pallas kernels, body(): pl.pallas_call(functools.partial(kernel, C, H), out_shape=jax.ShapeDtypeS...  57.3 us
    unnamed x1, local copies, waits for them, and re-layouts  1.82 us

profile of v3, /device:TPU:11, one launch (start us, length us, event | category | flops | bytes accessed | tf_op | source)
XLA Modules:
  0.0 59.1 jit_solution(12416544184375444739)
XLA Ops:
  0.0 57.3 %shard_map.91 = bf16[128,1792]{1,0:T(8,128)(2,1)} custom-call(bf16[128,1792]{1,0:T(8,128)(2,1)} %hid.1, bf16[128,1536]{1,0:T(8,128)(2,1)} %ql.1, bf16[576,1792]{1,0:T(8,128)(2,1)} %bitcast.2, f32[1,512]{1,0:T(1,128)} %bitcast.3, bf16[1536,3072]{1,0:T(8,128)(2,1)} %wq.1, bf16[512,4096]{1,0:T(8,128)(2,1)} %wkv.1, bf16[2048,1792]{1,0:T(8,128)(2,1)} %wo.1, ...), custom_call_target="tpu_custom_call" | custom-call | tf_op jit(solution)/shard_map/pallas_call | solution.py:324
  57.3 1.8 %copy.11 = bf16[128,1792]{1,0:T(8,128)(2,1)} copy(bf16[128,1792]{1,0:T(8,128)(2,1)} %shard_map.91) | data formatting | bytes 917504
